TPU v7x, 32 devices: a whole 2x2x4 slice. The times are simulated.
32 devices in a mesh: worker: 1, fsdp: 32 (over z, y, x, core).
Axes of the slice: x: 2, y: 2, z: 4, core: 2. Of those that a mesh axis runs over, the one named last changes fastest.
Arguments:
- inputs: bfloat16 [1, 2, 4096, 8192], P('worker', None, 'fsdp'), may hold values from -6 to 6
- targets: bfloat16 [1, 2, 4096, 512], P('worker', None, 'fsdp'), may hold values from -6 to 6
- base: float32 [8192, 512], P('fsdp', 'worker'), may hold values from -6 to 6
- adapter_a: float32 [1, 64, 8192], P('worker', None, 'fsdp'), may hold values from -6 to 6
- adapter_b: float32 [1, 512, 64], P('worker'), may hold values from -3 to 3
Outputs:
- new_base: float32 [8192, 512], P('fsdp', 'worker')
- final_a: float32 [1, 64, 8192], P('worker', None, 'fsdp')
- final_b: float32 [1, 512, 64], P('worker')
All inputs are finite; a program needn't handle non-finite values.
Results may differ from a plain program's by a relative error of at most 0.0048.
Values may be sent and summed in bfloat16 or wider, within the bound.
A program may use at most 64 MiB of HBM per device.

v0:
```python
import jax
import jax.numpy as jnp
from jax import lax
from jax.sharding import PartitionSpec as P

branch_scale = 0.25
rate_down = 200.0
rate_up = 20.0


def local(inputs, targets, base, adapter_a, adapter_b):
    high = lax.Precision.HIGHEST
    tokens = inputs[0]
    wanted = targets[0].astype(jnp.float32)
    a_start = adapter_a[0]
    b_start = adapter_b[0]
    steps, rows, width = tokens.shape
    features = b_start.shape[0]
    scale = width ** (-0.5)
    total_rows = float(rows * lax.axis_size("fsdp"))
    flat = tokens.reshape(steps * rows, width)
    base_half = base.astype(jnp.bfloat16)
    widened = lax.all_gather(base_half, "worker", axis=1, tiled=True)
    keys_flat = jnp.dot(
        flat,
        lax.all_gather(widened, "fsdp", axis=0, tiled=True),
        preferred_element_type=jnp.float32,
    )
    keys_base = (keys_flat * scale).reshape(steps, rows, features)
    shard = a_start.shape[1]
    offset = lax.axis_index("fsdp") * shard
    adapter = a_start
    upper = b_start
    exact = lax.all_gather(a_start, "fsdp", axis=1, tiled=True)
    a_half = exact.astype(jnp.bfloat16)
    for step in range(steps):
        current = tokens[step]
        low = jnp.einsum("td,rd->tr", current, a_half, preferred_element_type=jnp.float32) * scale
        output = keys_base[step] + branch_scale * jnp.dot(low, upper.T, precision=high)
        error = (output - wanted[step]) / total_rows
        b_part = branch_scale * jnp.dot(error.T, low, precision=high)
        back = (branch_scale * jnp.dot(error, upper, precision=high)).astype(jnp.bfloat16)
        a_part = jnp.dot(back.T, current, preferred_element_type=jnp.float32) * scale
        if step + 1 < steps:
            grad_b, grad_whole = lax.psum((b_part, a_part), "fsdp")
            exact = exact - rate_down * grad_whole
            adapter = lax.dynamic_slice_in_dim(exact, offset, shard, 1)
            a_half = exact.astype(jnp.bfloat16)
        else:
            grad_b = lax.psum(b_part, "fsdp")
            adapter = adapter - rate_down * lax.psum_scatter(
                a_part, "fsdp", scatter_dimension=1, tiled=True
            )
        upper = upper - rate_up * grad_b
    change = branch_scale * (
        jnp.dot(adapter.T, upper.T, precision=high) - jnp.dot(a_start.T, b_start.T, precision=high)
    )
    merged = lax.psum(change, "worker")
    columns = base.shape[1]
    own_part = lax.dynamic_slice_in_dim(merged, lax.axis_index("worker") * columns, columns, 1)
    new_base = base + own_part / lax.axis_size("worker")
    return (new_base, adapter[None], upper[None])


def solution(mesh):
    return jax.shard_map(
        local,
        mesh=mesh,
        in_specs=(
            P("worker", None, "fsdp", None),
            P("worker", None, "fsdp", None),
            P("fsdp", "worker"),
            P("worker", None, "fsdp"),
            P("worker", None, None),
        ),
        out_specs=(P("fsdp", "worker"), P("worker", None, "fsdp"), P("worker", None, None)),
        check_vma=False,
    )
```

profile of v0, /device:TPU:0, one launch (start us, length us, event | category | flops | bytes accessed | tf_op | source)
XLA Modules:
  0.0 569.4 jit_solution(16521397668905814728)
XLA Ops:
  7.2 0.0 all-gather.6.cloned.1.call-start
  7.2 0.7 all-gather.6.cloned.1.call-update
  7.9 0.0 all-gather.4.cloned.1.call-start
  7.9 1.8 convert_element_type.19
  9.7 0.0 all-gather.4.cloned.1.call-update
  9.7 0.0 all-reduce.6.cloned.1.call-start
  9.8 1.0 convert_element_type.21
  10.8 57.8 %all-gather.6.cloned.1.call-done = f32[1,64,8192]{2,1,0:T(8,128)} async-done(((f32[1,64,256]{2,1,0:T(8,128)}), f32[1,64,8192]{2,1,0:T(8,128)}) %all-gather.6.cloned.1.call-update) | async-done | bytes 2097168 | tf_op jit(solution)/shard_map/all_gather | solution.py:34
  68.6 3.1 fusion.20
  71.7 76.9 %all-gather.4.cloned.1.call-done = bf16[8192,512]{1,0:T(8,128)(2,1)} async-done(((bf16[256,512]{1,0:T(8,128)(2,1)}), bf16[8192,512]{1,0:T(8,128)(2,1)}) %all-gather.4.cloned.1.call-update) | async-done | bytes 8388624 | tf_op jit(solution)/shard_map/all_gather | solution.py:26
  148.6 0.0 copy-start.3
  148.6 0.0 copy-start
  148.6 7.1 %convolution_multiply_fusion.2 = f32[256,512]{1,0:T(8,128)S(1)} fusion(bf16[256,8192]{1,0:T(8,128)(2,1)} %bitcast.65, bf16[8192,512]{1,0:T(8,128)(2,1)} %all-gather.4.cloned.1.call-done), kind=kOutput, calls=%fused_computation.17 | convolution fusion | flops 2147614720 | bytes 13107200 | tf_op jit(solution)/shard_map/dot_general | solution.py:24
  155.7 0.0 copy-done.3
  155.7 0.0 copy-start.4
  155.8 0.4 fusion.16
  156.2 1.0 convolution_multiply_fusion.6
  157.2 0.4 fusion.18
  157.5 0.0 copy-done.4
  157.5 0.0 copy-done
  157.6 1.8 convolution_multiply_fusion.1
  159.4 0.0 all-reduce.6.cloned.1.call-update
  159.4 0.0 all-reduce.4.cloned.1.call-start
  159.5 133.8 %all-reduce.6.cloned.1.call-done = (f32[512,64]{0,1:T(8,128)}, f32[64,8192]{1,0:T(8,128)}) async-done(((f32[512,64]{0,1:T(8,128)}, f32[64,8192]{1,0:T(8,128)}), (f32[512,64]{0,1:T(8,128)}, f32[64,8192]{1,0:T(8,128)})) %all-reduce.6.cloned.1.call-update) | async-done | bytes 2228240 | tf_op jit(solution)/shard_map/psum | solution.py:45
  293.3 0.0 copy-start.1
  293.3 2.6 bitcast_subtract_fusion
  295.9 0.9 copy-done.1
  296.7 0.0 copy-start.8
  296.7 0.0 copy-start.5
  296.7 0.9 fusion.23
  297.6 0.0 copy-done.8
  297.7 0.2 copy-done.5
  297.8 0.4 fusion.17
  298.3 0.9 convolution_multiply_fusion.5
  299.2 0.4 fusion.19
  299.6 0.0 all-reduce.4.cloned.1.call-update
  299.6 0.0 reduce-scatter.2.cloned.1.call-start
  299.7 3.4 convolution_multiply_fusion
  303.1 0.0 copy-start.2
  303.1 0.0 copy-start.6
  303.1 0.0 reduce-scatter.2.cloned.1.call-update
  303.2 118.4 %all-reduce.4.cloned.1.call-done = f32[512,64]{0,1:T(8,128)} async-done(((f32[512,64]{0,1:T(8,128)}), f32[512,64]{0,1:T(8,128)}) %all-reduce.4.cloned.1.call-update) | async-done | bytes 131088 | tf_op jit(solution)/shard_map/psum | solution.py:50
  421.6 1.6 fusion.31
  423.2 136.0 %reduce-scatter.2.cloned.1.call-done = f32[64,256]{1,0:T(8,128)} async-done(((f32[64,8192]{1,0:T(8,128)}), f32[64,256]{1,0:T(8,128)}) %reduce-scatter.2.cloned.1.call-update) | async-done | bytes 65552 | tf_op jit(solution)/shard_map/reduce_scatter | solution.py:51
  559.2 0.0 copy-start.7
  559.2 1.6 fusion.32
  560.8 0.0 copy-done.2
  560.8 0.0 copy-done.6
  560.8 1.5 fusion.11
  562.2 0.0 copy-done.7
  562.3 0.6 fusion.33
  (1 shorter events, 0.0 us)
Async XLA Ops:
  7.2 61.5 %all-gather.6.cloned.1.call-start = ((), (), s32[]{:S(2)}) async-start(), calls=%async_computation.4 | async-start | bytes 2162688 | tf_op jit(solution)/shard_map/all_gather | solution.py:34
  7.9 140.7 %all-gather.4.cloned.1.call-start = ((), (), s32[]{:S(2)}) async-start(), calls=%async_computation.1 | async-start | bytes 8650752 | tf_op jit(solution)/shard_map/all_gather | solution.py:26
  9.7 283.5 %all-reduce.6.cloned.1.call-start = ((), (), s32[]{:S(2)}) async-start(), calls=%async_computation.5 | async-start | bytes 4456448 | tf_op jit(solution)/shard_map/psum | solution.py:45
  148.6 7.1 %copy-start.3 = (f32[1,512,64]{1,2,0:T(8,128)S(1)}, f32[1,512,64]{1,2,0:T(8,128)}, u32[]{:S(2)}) copy-start(f32[1,512,64]{1,2,0:T(8,128)} %param.9) | copy-start | bytes 393220
  148.6 8.9 %copy-start = (bf16[1,2,128,8192]{3,2,1,0:T(8,128)(2,1)S(1)}, bf16[1,2,128,8192]{3,2,1,0:T(8,128)(2,1)}, u32[]{:S(2)}) copy-start(bf16[1,2,128,8192]{3,2,1,0:T(8,128)(2,1)} %param.5) | copy-start | bytes 12582916
  155.7 1.8 copy-start.4
  159.4 262.2 %all-reduce.4.cloned.1.call-start = ((), (), s32[]{:S(2)}) async-start(), calls=%async_computation.3 | async-start | bytes 262144 | tf_op jit(solution)/shard_map/psum | solution.py:50
  293.3 3.4 copy-start.1
  296.7 0.9 copy-start.8
  296.7 1.1 copy-start.5
  299.6 259.5 %reduce-scatter.2.cloned.1.call-start = ((), (), s32[]{:S(2)}) async-start(), calls=%async_computation.2 | async-start | bytes 2162688 | tf_op jit(solution)/shard_map/reduce_scatter | solution.py:51
  303.1 257.6 %copy-start.2 = (f32[256,512]{1,0:T(8,128)S(1)}, f32[256,512]{1,0:T(8,128)}, u32[]{:S(2)}) copy-start(f32[256,512]{1,0:T(8,128)} %param.7) | copy-start | bytes 1572868
  303.1 257.6 %copy-start.6 = (f32[1,64,256]{2,1,0:T(8,128)S(1)}, f32[1,64,256]{2,1,0:T(8,128)}, u32[]{:S(2)}) copy-start(f32[1,64,256]{2,1,0:T(8,128)} %param.8) | copy-start | bytes 196612
  559.2 3.1 copy-start.7
Sparse Core Ops, SparseCore 0:
  10.9 57.6 all-gather.5
  72.1 76.5 all-gather.3
  159.5 133.7 all-reduce.5
  300.2 121.3 all-reduce.3
  423.8 135.3 reduce-scatter.1
where the time goes:
time: 570 us; the launch traced here: 569 us
  waiting for transfers between devices  524 us (92%)
  matrix products  22.9 us (4%)
  between operations  13.9 us (2%)
  other arithmetic  7.6 us (1%)
    reduce_scatter x1, waiting for transfers between devices, local(): lax.psum_scatter(a_part, 'fsdp', scatter_dimension=1, tiled=True)  136 us
    psum x1, waiting for transfers between devices, local(): grad_b, grad_whole = lax.psum((b_part, a_part), 'fsdp')  134 us
    psum x1, waiting for transfers between devices, local(): grad_b = lax.psum(b_part, 'fsdp')  118 us
    all_gather x1, waiting for transfers between devices, local(): lax.all_gather(widened, 'fsdp', axis=0, tiled=True)  76.9 us
    all_gather x1, waiting for transfers between devices, local(): exact = lax.all_gather(a_start, 'fsdp', axis=1, tiled=True)  57.8 us
  transfers between devices with their start and end apart: 5, of which 5 were waited for; matrix products, arithmetic and copies ran while one was open for 2% of the time, Pallas kernels for 0%

commit v1 on v0

v1 whole, which is shorter than its diff:
```python
import functools
import itertools

import jax
import jax.numpy as jnp
from jax import lax
from jax.experimental import pallas as pl
from jax.experimental.pallas import tpu as pltpu
from jax.sharding import PartitionSpec as P

branch_scale = 0.25
rate_down = 200.0
rate_up = 20.0
MESH = pl.DeviceIdType.MESH
f32 = jnp.float32
bf16 = jnp.bfloat16


def nn(a, b):
    return jnp.dot(a, b, preferred_element_type=f32)


def nt(a, b):
    return lax.dot_general(a, b, (((1,), (1,)), ((), ())), preferred_element_type=f32)


def exact(a, b, dims):
    return lax.dot_general(a, b, (dims, ((), ())), precision=lax.Precision.HIGHEST, preferred_element_type=f32)


def split(a):
    high = a.astype(bf16)
    return high, (a - high.astype(f32)).astype(bf16)


def together(*tasks):
    results = [None] * len(tasks)
    live = dict(enumerate(tasks))
    while live:
        for i in list(live):
            try:
                next(live[i])
            except StopIteration as stop:
                results[i] = stop.value
                del live[i]
    return results


def kernel(
    nz, add_base, x_hbm, y_ref, base_ref, a_ref, b_ref,
    nb_ref, fa_ref, fb_ref,
    x, g, keep, send_c, recv_c, send_xy, recv_xy, send_z, recv_z,
    ar, ar_c, ar_xy, ar_z, ar_fin, send_sem, recv_sem, local_sem,
):
    me = lax.axis_index("fsdp")
    c, q, z = me % 2, (me // 2) % 4, me // 8
    qx, qy = q % 2, q // 2
    steps, rows, width = x.shape
    rank, shard = a_ref.shape
    scale = width ** (-0.5)
    total_rows = float(rows * 8 * nz)

    def device(zz, qq, cc):
        return {"fsdp": (zz * 4 + qq) * 2 + cc}

    def near(m):
        return (1 - qy if m & 2 else qy) * 2 + (1 - qx if m & 1 else qx)

    def up(k):
        return (z + k) % nz

    def down(k):
        return (z + nz - k) % nz

    core_peer = device(z, q, 1 - c)
    serial = itertools.count()
    sent = []

    def send(src, dst, peer, lands):
        i = next(serial)
        copy = pltpu.make_async_remote_copy(
            src_ref=src, dst_ref=dst, send_sem=send_sem.at[i], recv_sem=recv_sem.at[i],
            device_id=peer, device_id_type=MESH,
        )
        copy.start()
        sent.append(copy)
        return pltpu.make_async_remote_copy(
            src_ref=lands, dst_ref=lands, send_sem=send_sem.at[i], recv_sem=recv_sem.at[i],
            device_id=peer, device_id_type=MESH,
        )

    loads = [pltpu.make_async_copy(x_hbm.at[j], x.at[j], local_sem.at[j]) for j in range(steps)]
    for load in loads:
        load.start()

    barrier = pltpu.get_barrier_semaphore()
    peers = [core_peer] + [device(z, near(m), c) for m in (1, 2, 3)] + [device(up(k), q, c) for k in range(1, nz)]
    for peer in peers:
        pl.semaphore_signal(barrier, inc=1, device_id=peer, device_id_type=MESH)

    half = base_ref[...].astype(bf16)
    a_now = a_ref[...]
    b_now = b_ref[...]

    def lifted(b):
        high, low = split(b)
        return (nt(high, half) + nt(low, half)).astype(bf16)

    g[0, c, q, z, 0] = a_now.astype(bf16)
    g[0, c, q, z, 1] = lifted(b_now)
    pl.semaphore_wait(barrier, len(peers))

    def gather(step, first, count):
        part = pl.ds(first, count)

        def block(cc, qq, zz):
            return g.at[step, cc, qq, zz, part]

        def line(cc, qq):
            return g.at[step, cc, qq, :, part]

        from_z = [
            send(block(c, q, z), block(c, q, z), device(up(k), q, c), block(c, q, down(k))) for k in range(1, nz)
        ]
        from_xy = {m: [] for m in (1, 2, 3)}
        for k in range(nz):
            if k:
                yield
                from_z[k - 1].wait_recv()
            for m in (1, 2, 3):
                from_xy[m].append(
                    send(block(c, q, down(k)), block(c, q, down(k)), device(z, near(m), c), block(c, near(m), down(k)))
                )
        from_core = [send(line(c, q), line(c, q), core_peer, line(1 - c, q))]
        for m in (1, 2, 3):
            yield
            for arrival in from_xy[m]:
                arrival.wait_recv()
            from_core.append(send(line(c, near(m)), line(c, near(m)), core_peer, line(1 - c, near(m))))
        for arrival in from_core:
            yield
            arrival.wait_recv()

    def project(step, first, count):
        def body(i, total):
            for j in range(8):
                block = g[step, j % 2, j // 2, i, pl.ds(first, count)].reshape(count * rank, shard)
                columns = pl.ds(pl.multiple_of((i * 8 + j) * shard, shard), shard)
                total = total + nt(block, x[step, :, columns])
            return total

        return scale * lax.fori_loop(0, nz, body, jnp.zeros((count * rank, rows), f32))

    def scatter(step, part, left):
        def product(cc, qq, zz):
            d = (zz * 4 + qq) * 2 + cc
            return nn(left, x[step, :, pl.ds(pl.multiple_of(d * shard, shard), shard)])

        from_core = {}
        for m in (1, 2, 3, 0):
            for zz in range(nz):
                send_c[step, part, m, zz] = product(1 - c, near(m), zz).astype(bf16)
            spot = recv_c.at[step, part, m]
            from_core[m] = send(send_c.at[step, part, m], spot, core_peer, spot)
        for m in (1, 2, 3, 0):
            for zz in range(nz):
                keep[part, m, zz] = product(c, near(m), zz)
        yield
        from_xy = []
        for m in (1, 2, 3):
            from_core[m].wait_recv()
            send_xy[step, part, m - 1] = (keep[part, m] + recv_c[step, part, m].astype(f32)).astype(bf16)
            spot = recv_xy.at[step, part, m - 1]
            from_xy.append(send(send_xy.at[step, part, m - 1], spot, device(z, near(m), c), spot))
        from_core[0].wait_recv()
        yield
        for arrival in from_xy:
            arrival.wait_recv()

        def held(zz):
            value = keep[part, 0, zz] + recv_c[step, part, 0, zz].astype(f32)
            for m in (0, 1, 2):
                value = value + recv_xy[step, part, m, zz].astype(f32)
            return value

        from_z = []
        for k in range(1, nz):
            send_z[step, part, k - 1] = held(up(k)).astype(bf16)
            spot = recv_z.at[step, part, k - 1]
            from_z.append(send(send_z.at[step, part, k - 1], spot, device(up(k), q, c), spot))
        value = held(z)
        yield
        for k, arrival in enumerate(from_z):
            arrival.wait_recv()
            value = value + recv_z[step, part, k].astype(f32)
        return value

    def reduce(step, value):
        cut = rank // 2
        ar[step, 0] = value[:cut]
        ar[step, 1] = value[cut:]
        arrival = send(ar.at[step, 1 - c], ar_c.at[step], core_peer, ar_c.at[step])
        yield
        arrival.wait_recv()
        ar_xy[step, q] = (ar[step, c] + ar_c[step]).astype(bf16)
        arrivals = [
            send(ar_xy.at[step, q], ar_xy.at[step, q], device(z, near(m), c), ar_xy.at[step, near(m)])
            for m in (1, 2, 3)
        ]
        yield
        for arrival in arrivals:
            arrival.wait_recv()
        value = ar_xy[step, 0].astype(f32)
        for i in range(1, 4):
            value = value + ar_xy[step, i].astype(f32)
        ar_z[step, z] = value.astype(bf16)
        arrivals = [
            send(ar_z.at[step, z], ar_z.at[step, z], device(up(k), q, c), ar_z.at[step, down(k)])
            for k in range(1, nz)
        ]
        yield
        for arrival in arrivals:
            arrival.wait_recv()
        value = ar_z[step, 0].astype(f32)
        for i in range(1, nz):
            value = value + ar_z[step, i].astype(f32)
        ar_fin[step, c] = value
        arrival = send(ar_fin.at[step, c], ar_fin.at[step, c], core_peer, ar_fin.at[step, 1 - c])
        yield
        arrival.wait_recv()
        return jnp.concatenate([ar_fin[step, 0], ar_fin[step, 1]], axis=0)

    def back_of(step, low, lift, b):
        high, rest = split(b)
        wanted = nt(high, y_ref[step]) + nt(rest, y_ref[step])
        branch = exact(exact(b, b, ((1,), (1,))), low, ((1,), (0,)))
        return ((branch_scale / total_rows) * (lift + branch_scale * branch - wanted)).astype(bf16)

    def up_part(step, low, low_half, spread, b):
        high, rest = split(spread)
        keys = scale * (nn(high, half) + nn(rest, half))
        gram = exact(low_half.astype(f32), low, ((1,), (1,)))
        branch = branch_scale * exact(gram, b, ((1,), (0,)))
        return (branch_scale / total_rows) * (keys + branch - nn(low_half, y_ref[step]))

    state = {"b": b_now, "a": a_now}

    def up_chain(step, low, low_half):
        spread = yield from scatter(step, 0, low_half)
        value = up_part(step, low, low_half, spread, state["b"])
        grad = yield from reduce(step, value)
        state["b"] = state["b"] - rate_up * grad

    def down_chain(step, back):
        grad = yield from scatter(step, 1, back)
        state["a"] = state["a"] - (rate_down * scale) * grad

    together(gather(0, 0, 2))
    for load in loads:
        load.wait()
    both = project(0, 0, 2)
    low, lift = both[:rank], both[rank:]
    low_half = low.astype(bf16)
    back = back_of(0, low, lift, b_now)

    for step in range(steps):
        last = step + 1 == steps

        def first(step=step, low=low, low_half=low_half, last=last):
            yield from up_chain(step, low, low_half)
            if not last:
                g[step + 1, c, q, z, 1] = lifted(state["b"])
                yield from gather(step + 1, 1, 1)

        def second(step=step, back=back, last=last):
            yield from down_chain(step, back)
            if not last:
                g[step + 1, c, q, z, 0] = state["a"].astype(bf16)
                yield from gather(step + 1, 0, 1)
                return project(step + 1, 0, 1)

        _, low = together(first(), second())
        if not last:
            low_half = low.astype(bf16)
            back = back_of(step + 1, low, project(step + 1, 1, 1), state["b"])

    fa_ref[...] = state["a"]
    fb_ref[...] = state["b"]
    left = jnp.concatenate([state["a"], -a_now], axis=0).T
    right = jnp.concatenate([state["b"], b_now], axis=0)
    change = branch_scale * exact(left, right, ((1,), (0,)))
    nb_ref[...] = base_ref[...] + change if add_base else change
    for copy in sent:
        copy.wait_send()


def local(inputs, targets, base, adapter_a, adapter_b):
    n = lax.axis_size("fsdp")
    workers = lax.axis_size("worker")
    nz = n // 8
    tokens, wanted, a, b = inputs[0], targets[0], adapter_a[0], adapter_b[0].T
    steps, rows, width = tokens.shape
    rank, shard = a.shape
    features = b.shape[1]
    whole = base
    if workers > 1:
        whole = lax.all_gather(base.astype(bf16), "worker", axis=1, tiled=True).astype(f32)
    vmem = pl.BlockSpec(memory_space=pltpu.VMEM)
    block = (rank, shard)
    cut = (rank // 2, features)
    nzs = max(nz - 1, 1)
    per_gather = (nz - 1) + 3 * nz + 4
    messages = (2 * steps - 1) * per_gather + 2 * steps * (7 + nz - 1) + steps * (5 + nz - 1)
    merged, final_a, final_b = pl.pallas_call(
        functools.partial(kernel, nz, workers == 1),
        out_shape=(
            jax.ShapeDtypeStruct((shard, features), f32),
            jax.ShapeDtypeStruct(block, f32),
            jax.ShapeDtypeStruct((rank, features), f32),
        ),
        in_specs=[pl.BlockSpec(memory_space=pl.ANY)] + [vmem] * 4,
        out_specs=(vmem, vmem, vmem),
        scratch_shapes=[
            pltpu.VMEM((steps, rows, width), bf16),
            pltpu.VMEM((steps, 2, 4, nz, 2) + block, bf16),
            pltpu.VMEM((2, 4, nz) + block, f32),
            pltpu.VMEM((steps, 2, 4, nz) + block, bf16),
            pltpu.VMEM((steps, 2, 4, nz) + block, bf16),
            pltpu.VMEM((steps, 2, 3, nz) + block, bf16),
            pltpu.VMEM((steps, 2, 3, nz) + block, bf16),
            pltpu.VMEM((steps, 2, nzs) + block, bf16),
            pltpu.VMEM((steps, 2, nzs) + block, bf16),
            pltpu.VMEM((steps, 2) + cut, f32),
            pltpu.VMEM((steps,) + cut, f32),
            pltpu.VMEM((steps, 4) + cut, bf16),
            pltpu.VMEM((steps, nz) + cut, bf16),
            pltpu.VMEM((steps, 2) + cut, f32),
            pltpu.SemaphoreType.DMA((messages,)),
            pltpu.SemaphoreType.DMA((messages,)),
            pltpu.SemaphoreType.DMA((steps,)),
        ],
        compiler_params=pltpu.CompilerParams(
            collective_id=0, has_side_effects=True, vmem_limit_bytes=48 * 1024 * 1024
        ),
    )(tokens, wanted, whole, a, b)
    if workers > 1:
        share = lax.psum_scatter(merged, "worker", scatter_dimension=1, tiled=True)
        merged = base + share / workers
    return (merged, final_a[None], final_b.T[None])


def solution(mesh):
    return jax.shard_map(
        local,
        mesh=mesh,
        in_specs=(
            P("worker", None, "fsdp", None),
            P("worker", None, "fsdp", None),
            P("fsdp", "worker"),
            P("worker", None, "fsdp"),
            P("worker", None, None),
        ),
        out_specs=(P("fsdp", "worker"), P("worker", None, "fsdp"), P("worker", None, None)),
        check_vma=False,
    )
```

time: 570 us -> 106 us (0.19)
  waiting for transfers between devices: 524 us -> 0 us
  Pallas kernels: 0 us -> 96.4 us
  matrix products: 22.9 us -> 0 us
  between operations: 13.9 us -> 0.65 us
  other arithmetic: 7.6 us -> 0 us
  local copies, waits for them, and re-layouts: 1.11 us -> 7.99 us
    psum x2 -> x0, waiting for transfers between devices: 252 us -> none  [the longest x1 134 us: local(): grad_b, grad_whole = lax.psum((b_part, a_part), 'fsdp')]
    reduce_scatter x1 -> x0, waiting for transfers between devices: 136 us -> none  [local(): lax.psum_scatter(a_part, 'fsdp', scatter_dimension=1, tiled=True)]
    all_gather x2 -> x0, waiting for transfers between devices: 135 us -> none  [the longest x1 76.9 us: local(): lax.all_gather(widened, 'fsdp', axis=0, tiled=True)]
    pallas_call x0 -> x1, Pallas kernels: none -> 96.4 us  [local(): pl.pallas_call(functools.partial(kernel, nz, workers == 1), out_shape=(ja...]
    dot_general x13 -> x0, matrix products: 22.9 us -> none  [the longest x1 7.11 us: local(): jnp.dot(flat, lax.all_gather(widened, 'fsdp', axis=0, tiled=True), prefer...]
    unnamed x18 -> x13, local copies, waits for them, and re-layouts: 1.11 us -> 7.99 us
  transfers between devices with their start and end apart: 5 -> 0, of which waited for: 5 -> 0; matrix products, arithmetic and copies ran while one was open for 2% -> 0% of each run, Pallas kernels for 0% -> 0%
where the time goes in v1:
time: 106 us; the launch traced here: 105 us
  Pallas kernels  96.4 us (91%)
  local copies, waits for them, and re-layouts  7.99 us (8%)
    pallas_call x1, Pallas kernels, local(): pl.pallas_call(functools.partial(kernel, nz, workers == 1), out_shape=(ja...  96.4 us
    unnamed x13, local copies, waits for them, and re-layouts  7.99 us

profile of v1, /device:TPU:0, one launch (start us, length us, event | category | flops | bytes accessed | tf_op | source)
XLA Modules:
  0.0 105.1 jit_solution(3860127256503019795)
XLA Ops:
  0.6 0.0 copy-start
  0.6 2.2 %copy-done = bf16[1,2,128,8192]{3,2,1,0:T(8,128)(2,1)S(1)} copy-done((bf16[1,2,128,8192]{3,2,1,0:T(8,128)(2,1)S(1)}, bf16[1,2,128,8192]{3,2,1,0:T(8,128)(2,1)}, u32[]{:S(2)}) %copy-start) | copy-done | bytes 4194328
  2.8 0.0 copy-start.1
  2.8 1.0 copy-done.1
  3.9 0.0 copy-start.2
  3.9 0.9 copy-done.2
  4.8 0.0 copy-start.3
  4.8 0.9 copy-done.3
  5.7 0.0 copy-start.4
  5.7 0.8 copy-done.4
  6.6 96.4 %shard_map.76 = (f32[256,512]{1,0:T(8,128)S(1)}, f32[64,256]{1,0:T(8,128)S(1)}, f32[64,512]{1,0:T(8,128)S(1)}) custom-call(bf16[2,128,8192]{2,1,0:T(8,128)(2,1)S(1)} %bitcast.10, bf16[2,128,512]{2,1,0:T(8,128)(2,1)S(1)} %bitcast.11, f32[256,512]{1,0:T(8,128)S(1)} %copy-done.1, f32[64,256]{1,0:T(8,128)S(1)} %bitcast.14, f32[64,512]{1,0:T(8,128)S(1)} %bitcast.12), custom_call_target="tpu_custom_call" | custom-call | tf_op jit(solution)/shard_map/pallas_call | solution.py:314
  103.0 0.8 copy.11
  103.8 0.6 copy.12
  104.4 0.7 copy.13
Async XLA Ops:
  0.6 2.2 %copy-start = (bf16[1,2,128,8192]{3,2,1,0:T(8,128)(2,1)S(1)}, bf16[1,2,128,8192]{3,2,1,0:T(8,128)(2,1)}, u32[]{:S(2)}) copy-start(bf16[1,2,128,8192]{3,2,1,0:T(8,128)(2,1)} %param.5) | copy-start | bytes 12582916
  2.8 1.0 copy-start.1
  3.9 0.9 copy-start.2
  4.8 0.9 copy-start.3
  5.7 0.8 copy-start.4

commit v2 on v1

--- a/solution.py
+++ b/solution.py
@@ -12,6 +12,7 @@
 rate_down = 200.0
 rate_up = 20.0
 MESH = pl.DeviceIdType.MESH
+ORDER = "0101001"
 f32 = jnp.float32
 bf16 = jnp.bfloat16
 
@@ -33,24 +34,21 @@
     return high, (a - high.astype(f32)).astype(bf16)
 
 
-def together(*tasks):
-    results = [None] * len(tasks)
+def together(tasks, order=""):
     live = dict(enumerate(tasks))
+    turns = [int(turn) for turn in order]
     while live:
-        for i in list(live):
-            try:
-                next(live[i])
-            except StopIteration as stop:
-                results[i] = stop.value
+        for i in turns or list(live):
+            if i in live and next(live[i], True):
                 del live[i]
-    return results
+        turns = []
 
 
 def kernel(
-    nz, add_base, x_hbm, y_ref, base_ref, a_ref, b_ref,
+    nz, add_base, x_hbm, y_hbm, base_hbm, a_hbm, b_hbm,
     nb_ref, fa_ref, fb_ref,
-    x, g, keep, send_c, recv_c, send_xy, recv_xy, send_z, recv_z,
-    ar, ar_c, ar_xy, ar_z, ar_fin, send_sem, recv_sem, local_sem,
+    x, y_ref, base_ref, a_ref, b_ref, g, keep, send_c, recv_c, send_xy, recv_xy, send_z, recv_z,
+    ar, ar_in, ar_z, ar_fin, send_sem, recv_sem, local_sem,
 ):
     me = lax.axis_index("fsdp")
     c, q, z = me % 2, (me // 2) % 4, me // 8
@@ -89,15 +87,24 @@
             device_id=peer, device_id_type=MESH,
         )
 
-    loads = [pltpu.make_async_copy(x_hbm.at[j], x.at[j], local_sem.at[j]) for j in range(steps)]
+    pairs = [(base_hbm, base_ref), (b_hbm, b_ref), (a_hbm, a_ref)]
+    pairs += [(x_hbm.at[j], x.at[j]) for j in range(steps)] + [(y_hbm, y_ref)]
+    loads = [pltpu.make_async_copy(src, dst, local_sem.at[j]) for j, (src, dst) in enumerate(pairs)]
     for load in loads:
         load.start()
 
     barrier = pltpu.get_barrier_semaphore()
-    peers = [core_peer] + [device(z, near(m), c) for m in (1, 2, 3)] + [device(up(k), q, c) for k in range(1, nz)]
+    cell = [(m, flip) for flip in (0, 1) for m in range(4)][1:]
+
+    def member(m, flip):
+        return near(m), 1 - c if flip else c
+
+    peers = [device(z, *member(m, flip)) for m, flip in cell] + [device(up(k), q, c) for k in range(1, nz)]
     for peer in peers:
         pl.semaphore_signal(barrier, inc=1, device_id=peer, device_id_type=MESH)
 
+    for load in loads[:3]:
+        load.wait()
     half = base_ref[...].astype(bf16)
     a_now = a_ref[...]
     b_now = b_ref[...]
@@ -196,24 +203,19 @@
         return value
 
     def reduce(step, value):
-        cut = rank // 2
-        ar[step, 0] = value[:cut]
-        ar[step, 1] = value[cut:]
-        arrival = send(ar.at[step, 1 - c], ar_c.at[step], core_peer, ar_c.at[step])
-        yield
-        arrival.wait_recv()
-        ar_xy[step, q] = (ar[step, c] + ar_c[step]).astype(bf16)
-        arrivals = [
-            send(ar_xy.at[step, q], ar_xy.at[step, q], device(z, near(m), c), ar_xy.at[step, near(m)])
-            for m in (1, 2, 3)
-        ]
-        yield
-        for arrival in arrivals:
-            arrival.wait_recv()
-        value = ar_xy[step, 0].astype(f32)
-        for i in range(1, 4):
-            value = value + ar_xy[step, i].astype(f32)
-        ar_z[step, z] = value.astype(bf16)
+        ar[step] = value.reshape(ar.shape[1:])
+        place = q * 2 + c
+        arrivals = []
+        for i, (m, flip) in enumerate(cell):
+            qq, cc = member(m, flip)
+            spot = ar_in.at[step, i]
+            arrivals.append(send(ar.at[step, qq * 2 + cc], spot, device(z, qq, cc), spot))
+        yield
+        value = ar[step, place]
+        for i, arrival in enumerate(arrivals):
+            arrival.wait_recv()
+            value = value + ar_in[step, i]
+        ar_z[step, z] = value
         arrivals = [
             send(ar_z.at[step, z], ar_z.at[step, z], device(up(k), q, c), ar_z.at[step, down(k)])
             for k in range(1, nz)
@@ -221,14 +223,19 @@
         yield
         for arrival in arrivals:
             arrival.wait_recv()
-        value = ar_z[step, 0].astype(f32)
+        value = ar_z[step, 0]
         for i in range(1, nz):
-            value = value + ar_z[step, i].astype(f32)
-        ar_fin[step, c] = value
-        arrival = send(ar_fin.at[step, c], ar_fin.at[step, c], core_peer, ar_fin.at[step, 1 - c])
-        yield
-        arrival.wait_recv()
-        return jnp.concatenate([ar_fin[step, 0], ar_fin[step, 1]], axis=0)
+            value = value + ar_z[step, i]
+        ar_fin[step, place] = value
+        arrivals = []
+        for m, flip in cell:
+            qq, cc = member(m, flip)
+            own = ar_fin.at[step, place]
+            arrivals.append(send(own, own, device(z, qq, cc), ar_fin.at[step, qq * 2 + cc]))
+        yield
+        for arrival in arrivals:
+            arrival.wait_recv()
+        return ar_fin[step].reshape(rank, -1)
 
     def back_of(step, low, lift, b):
         high, rest = split(b)
@@ -243,51 +250,69 @@
         branch = branch_scale * exact(gram, b, ((1,), (0,)))
         return (branch_scale / total_rows) * (keys + branch - nn(low_half, y_ref[step]))
 
-    state = {"b": b_now, "a": a_now}
-
-    def up_chain(step, low, low_half):
+    state = {("b", 0): b_now, ("a", 0): a_now}
+
+    def ready(*key):
+        while key not in state:
+            yield
+
+    def up_chain(step):
+        yield from ready("low", step)
+        low = state["low", step]
+        low_half = low.astype(bf16)
         spread = yield from scatter(step, 0, low_half)
-        value = up_part(step, low, low_half, spread, state["b"])
-        grad = yield from reduce(step, value)
-        state["b"] = state["b"] - rate_up * grad
-
-    def down_chain(step, back):
+        yield from ready("b", step)
+        b = state["b", step]
+        grad = yield from reduce(step, up_part(step, low, low_half, spread, b))
+        state["b", step + 1] = b - rate_up * grad
+
+    def lift_chain(step):
+        g[step, c, q, z, 1] = lifted(state["b", step])
+        yield from gather(step, 1, 1)
+        state["lift", step] = project(step, 1, 1)
+
+    def down_chain(step):
+        yield from ready("lift", step)
+        yield from ready("low", step)
+        back = back_of(step, state["low", step], state["lift", step], state["b", step])
         grad = yield from scatter(step, 1, back)
-        state["a"] = state["a"] - (rate_down * scale) * grad
-
-    together(gather(0, 0, 2))
-    for load in loads:
+        state["a", step + 1] = state["a", step] - (rate_down * scale) * grad
+
+    def low_chain(step):
+        g[step, c, q, z, 0] = state["a", step].astype(bf16)
+        yield from gather(step, 0, 1)
+        state["low", step] = project(step, 0, 1)
+
+    def first():
+        for step in range(0, steps, 2):
+            yield from up_chain(step)
+            if step + 1 < steps:
+                yield from lift_chain(step + 1)
+                yield from down_chain(step + 1)
+            if step + 2 < steps:
+                yield from low_chain(step + 2)
+
+    def second():
+        for step in range(0, steps, 2):
+            yield from down_chain(step)
+            if step + 1 < steps:
+                yield from low_chain(step + 1)
+                yield from up_chain(step + 1)
+            if step + 2 < steps:
+                yield from lift_chain(step + 2)
+
+    together([gather(0, 0, 2)])
+    for load in loads[3:]:
         load.wait()
     both = project(0, 0, 2)
-    low, lift = both[:rank], both[rank:]
-    low_half = low.astype(bf16)
-    back = back_of(0, low, lift, b_now)
-
-    for step in range(steps):
-        last = step + 1 == steps
-
-        def first(step=step, low=low, low_half=low_half, last=last):
-            yield from up_chain(step, low, low_half)
-            if not last:
-                g[step + 1, c, q, z, 1] = lifted(state["b"])
-                yield from gather(step + 1, 1, 1)
-
-        def second(step=step, back=back, last=last):
-            yield from down_chain(step, back)
-            if not last:
-                g[step + 1, c, q, z, 0] = state["a"].astype(bf16)
-                yield from gather(step + 1, 0, 1)
-                return project(step + 1, 0, 1)
-
-        _, low = together(first(), second())
-        if not last:
-            low_half = low.astype(bf16)
-            back = back_of(step + 1, low, project(step + 1, 1, 1), state["b"])
-
-    fa_ref[...] = state["a"]
-    fb_ref[...] = state["b"]
-    left = jnp.concatenate([state["a"], -a_now], axis=0).T
-    right = jnp.concatenate([state["b"], b_now], axis=0)
+    state["low", 0], state["lift", 0] = both[:rank], both[rank:]
+    together([first(), second()], ORDER)
+    a_end, b_end = state["a", steps], state["b", steps]
+
+    fa_ref[...] = a_end
+    fb_ref[...] = b_end
+    left = jnp.concatenate([a_end, -a_now], axis=0).T
+    right = jnp.concatenate([b_end, b_now], axis=0)
     change = branch_scale * exact(left, right, ((1,), (0,)))
     nb_ref[...] = base_ref[...] + change if add_base else change
     for copy in sent:
@@ -307,10 +332,10 @@
         whole = lax.all_gather(base.astype(bf16), "worker", axis=1, tiled=True).astype(f32)
     vmem = pl.BlockSpec(memory_space=pltpu.VMEM)
     block = (rank, shard)
-    cut = (rank // 2, features)
+    cut = (rank // 8, features)
     nzs = max(nz - 1, 1)
     per_gather = (nz - 1) + 3 * nz + 4
-    messages = (2 * steps - 1) * per_gather + 2 * steps * (7 + nz - 1) + steps * (5 + nz - 1)
+    messages = (2 * steps - 1) * per_gather + 2 * steps * (7 + nz - 1) + steps * (14 + nz - 1)
     merged, final_a, final_b = pl.pallas_call(
         functools.partial(kernel, nz, workers == 1),
         out_shape=(
@@ -318,10 +343,14 @@
             jax.ShapeDtypeStruct(block, f32),
             jax.ShapeDtypeStruct((rank, features), f32),
         ),
-        in_specs=[pl.BlockSpec(memory_space=pl.ANY)] + [vmem] * 4,
+        in_specs=[pl.BlockSpec(memory_space=pl.ANY)] * 5,
         out_specs=(vmem, vmem, vmem),
         scratch_shapes=[
             pltpu.VMEM((steps, rows, width), bf16),
+            pltpu.VMEM(wanted.shape, bf16),
+            pltpu.VMEM((shard, features), f32),
+            pltpu.VMEM(block, f32),
+            pltpu.VMEM((rank, features), f32),
             pltpu.VMEM((steps, 2, 4, nz, 2) + block, bf16),
             pltpu.VMEM((2, 4, nz) + block, f32),
             pltpu.VMEM((steps, 2, 4, nz) + block, bf16),
@@ -330,17 +359,16 @@
             pltpu.VMEM((steps, 2, 3, nz) + block, bf16),
             pltpu.VMEM((steps, 2, nzs) + block, bf16),
             pltpu.VMEM((steps, 2, nzs) + block, bf16),
-            pltpu.VMEM((steps, 2) + cut, f32),
-            pltpu.VMEM((steps,) + cut, f32),
-            pltpu.VMEM((steps, 4) + cut, bf16),
-            pltpu.VMEM((steps, nz) + cut, bf16),
-            pltpu.VMEM((steps, 2) + cut, f32),
+            pltpu.VMEM((steps, 8) + cut, f32),
+            pltpu.VMEM((steps, 7) + cut, f32),
+            pltpu.VMEM((steps, nz) + cut, f32),
+            pltpu.VMEM((steps, 8) + cut, f32),
             pltpu.SemaphoreType.DMA((messages,)),
             pltpu.SemaphoreType.DMA((messages,)),
-            pltpu.SemaphoreType.DMA((steps,)),
+            pltpu.SemaphoreType.DMA((steps + 4,)),
         ],
         compiler_params=pltpu.CompilerParams(
-            collective_id=0, has_side_effects=True, vmem_limit_bytes=48 * 1024 * 1024
+            collective_id=0, has_side_effects=True, vmem_limit_bytes=60 * 1024 * 1024
         ),
     )(tokens, wanted, whole, a, b)
     if workers > 1:

time: 106 us -> 98.2 us (0.926)
  Pallas kernels: 96.4 us -> 92.4 us
  local copies, waits for them, and re-layouts: 7.99 us -> 4.91 us
    pallas_call x1, Pallas kernels: 96.4 us -> 92.4 us  [local(): pl.pallas_call(functools.partial(kernel, nz, workers == 1), out_shape=(ja...]
    unnamed x13 -> x3, local copies, waits for them, and re-layouts: 7.99 us -> 4.91 us
where the time goes in v2:
time: 98.2 us; the launch traced here: 97.9 us
  Pallas kernels  92.4 us (94%)
  local copies, waits for them, and re-layouts  4.91 us (5%)
    pallas_call x1, Pallas kernels, local(): pl.pallas_call(functools.partial(kernel, nz, workers == 1), out_shape=(ja...  92.4 us
    unnamed x3, local copies, waits for them, and re-layouts  4.91 us

profile of v2, /device:TPU:0, one launch (start us, length us, event | category | flops | bytes accessed | tf_op | source)
XLA Modules:
  0.0 97.9 jit_solution(14081804584771341883)
XLA Ops:
  0.6 92.4 %shard_map.76 = (f32[256,512]{1,0:T(8,128)}, f32[64,256]{1,0:T(8,128)}, f32[64,512]{1,0:T(8,128)}) custom-call(bf16[2,128,8192]{2,1,0:T(8,128)(2,1)} %bitcast.10, bf16[2,128,512]{2,1,0:T(8,128)(2,1)} %bitcast.11, f32[256,512]{1,0:T(8,128)} %base_hbm.1, f32[64,256]{1,0:T(8,128)} %bitcast.14, f32[64,512]{1,0:T(8,128)} %bitcast.12), custom_call_target="tpu_custom_call" | custom-call | tf_op jit(solution)/shard_map/pallas_call | solution.py:339
  93.0 1.9 %copy.11 = f32[256,512]{1,0:T(8,128)} copy(f32[256,512]{1,0:T(8,128)} %get-tuple-element.12) | data formatting | bytes 1048576
  94.9 1.5 %copy.12 = f32[1,64,256]{2,1,0:T(8,128)} copy(f32[1,64,256]{2,1,0:T(8,128)} %bitcast.15) | data formatting | bytes 131072
  96.4 1.6 %copy.13 = f32[1,512,64]{1,2,0:T(8,128)} copy(f32[1,512,64]{1,2,0:T(8,128)} %bitcast.13) | data formatting | bytes 262144
